TPU v7x, 32 devices: a whole 2x2x4 slice. The times are simulated.
32 devices in a mesh: dom: 8 (over z, y), sub: 4 (over x, core).
Axes of the slice: x: 2, y: 2, z: 4, core: 2. Of those that a mesh axis runs over, the one named last changes fastest.
Arguments:
- segments: float32 [64, 9, 128], P(('dom', 'sub')), may hold values from -6 to 6
- stress: float32 [3, 3], replicated, may hold values from -3 to 3
- drag_coef: float32 [64, 128], P(('dom', 'sub')), may hold values from 0.5 to 4
- send_ids: int32 [32, 8, 1], P(('dom', 'sub')), may hold values from -1 to 1, as said below
- partner_ids: int32 [32, 8, 1], P(('dom', 'sub')), may hold values from 0 to 1
Outputs:
- positions: float32 [64, 3, 128], P(('dom', 'sub'))
- velocity: float32 [64, 3, 128], P(('dom', 'sub'))
Inputs may be any that keep to these rules, and one draw needn't show every extreme that they name: `send_ids`: entry [d, p, s] names a block of device d, which goes in slot s to the device with dom index p and d's sub index; -1 marks an empty slot. Some device receives a block in every slot from every sender.
All inputs are finite; a program needn't handle non-finite values.
Results may differ from a plain program's by a relative error of at most 0.0003.
Values sent between devices are 32-bit elements; how exact they have to be, the bound alone decides.
A program may use at most 64 MiB of HBM per device.

v0:
```python
import functools

import jax
import jax.numpy as jnp
from jax import lax
from jax.experimental import pallas as pl
from jax.experimental.pallas import tpu as pltpu
from jax.sharding import PartitionSpec as P

STEPS = 2
COUPLE = 0.0625
CORE_SQUARE = 0.5
TENSION = 0.25
STEP_LENGTH = 1.0
EPSILON = 1e-06

MESH = pl.DeviceIdType.MESH
ROWS = 16
UNROLL_LIMIT = 64


def repeat(first, last, body):
    if last - first <= UNROLL_LIMIT:
        for index in range(first, last):
            body(index)
    else:

        def step(index, carry):
            body(index)
            return carry

        lax.fori_loop(first, last, step, 0)


def kernel(
    n_dom,
    n_sub,
    seg_ref,
    drag_ref,
    stress_ref,
    send_ref,
    partner_ref,
    pos_ref,
    vel_ref,
    top_ref,
    stage,
    held,
    numer,
    left_side,
    at_i,
    vel_i,
    acc,
    sources,
    applied_ref,
    drag8_ref,
    vel_tx,
    vel_rx,
    top1_tx,
    top1_rx,
    top2_tx,
    top2_rx,
    state_send,
    state_recv,
    vel_send,
    vel_recv,
    top1_send,
    top1_recv,
    top2_send,
    top2_recv,
):
    nb, _, width = seg_ref.shape
    slots = n_sub + n_dom - 1
    dom = lax.axis_index("dom")
    sub = lax.axis_index("sub")
    used = 3 * nb
    tail = nb * ROWS

    if n_dom <= UNROLL_LIMIT:
        dom_ids = [lax.rem(dom + k, n_dom) for k in range(n_dom)]
    sub_ids = [lax.rem(sub + k, n_sub) for k in range(n_sub)]

    def dom_id(k):
        return dom_ids[k] if isinstance(k, int) else lax.rem(dom + k, n_dom)

    def sub_id(k):
        return sub_ids[k] if isinstance(k, int) else lax.rem(sub + k, n_sub)

    barrier = pltpu.get_barrier_semaphore()

    def greet(dom_to, sub_to):
        pl.semaphore_signal(barrier, inc=1, device_id=(dom_to, sub_to), device_id_type=MESH)

    repeat(1, n_dom, lambda k: greet(dom_id(k), sub))
    repeat(1, n_sub, lambda k: greet(dom, sub_id(k)))

    held[0] = jnp.zeros((tail + 8, width), jnp.float32)
    for r in range(nb):
        for a in range(3):
            held[0, ROWS * r + 3 * a : ROWS * r + 3 * a + 3, :] = seg_ref[r, 6 + a : 7 + a, :] * seg_ref[r, 3:6, :]
        held[0, tail + 3 * r : tail + 3 * r + 3, :] = seg_ref[r, 0:3, :]
    products = [held[0, ROWS * r : ROWS * (r + 1), :] for r in range(nb)]
    position = held[0, tail : tail + 8, :]
    row_id = lax.broadcasted_iota(jnp.int32, (8, width), 0)
    lane = lax.broadcasted_iota(jnp.int32, (8, width), 1)

    def fill(q):
        sent = send_ref[0, q].astype(jnp.float32)
        partner = partner_ref[0, q].astype(jnp.float32)
        for r in range(nb):
            stage[q, ROWS * r : ROWS * (r + 1), :] = products[r]
        entries = jnp.where(row_id == used, sent, jnp.where(row_id == used + 1, partner, position))
        stage[q, tail : tail + 8, :] = entries

    repeat(0, n_dom, fill)

    def sub_copy(k):
        return pltpu.make_async_remote_copy(
            src_ref=held.at[0],
            dst_ref=held.at[k],
            send_sem=state_send.at[k],
            recv_sem=state_recv.at[k],
            device_id=(dom, sub_id(k)),
            device_id_type=MESH,
        )

    def dom_copy(k):
        slot = n_sub - 1 + k
        return pltpu.make_async_remote_copy(
            src_ref=stage.at[dom_id(k)],
            dst_ref=held.at[slot],
            send_sem=state_send.at[slot],
            recv_sem=state_recv.at[slot],
            device_id=(dom_id(k), sub),
            device_id_type=MESH,
        )

    pl.semaphore_wait(barrier, slots - 1)
    repeat(1, n_dom, lambda k: dom_copy(k).start())
    repeat(1, n_sub, lambda k: sub_copy(k).start())

    applied_ref[...] = jnp.zeros((8, width), jnp.float32)
    drag8_ref[...] = jnp.ones((8, width), jnp.float32)
    for o in range(nb):
        b = [seg_ref[o, 6 + c : 7 + c, :] for c in range(3)]
        ln = [seg_ref[o, 3 + c : 4 + c, :] for c in range(3)]
        pulled = [
            stress_ref[c, 0] * b[0] + stress_ref[c, 1] * b[1] + stress_ref[c, 2] * b[2] for c in range(3)
        ]
        applied_ref[3 * o : 3 * o + 1, :] = pulled[1] * ln[2] - pulled[2] * ln[1]
        applied_ref[3 * o + 1 : 3 * o + 2, :] = pulled[2] * ln[0] - pulled[0] * ln[2]
        applied_ref[3 * o + 2 : 3 * o + 3, :] = pulled[0] * ln[1] - pulled[1] * ln[0]
        for c in range(3):
            drag8_ref[3 * o + c : 3 * o + c + 1, :] = drag_ref[o : o + 1, :]

    def split(value):
        high = value.astype(jnp.bfloat16)
        low = (value - high.astype(jnp.float32)).astype(jnp.bfloat16)
        return high, low

    def spread(target, tile):
        turned = tile.T
        for row in range(used):
            target[row] = jnp.broadcast_to(turned[:, row : row + 1], (width, width))

    spread(at_i, position)
    for o in range(nb):
        high = products[o].astype(jnp.bfloat16).astype(jnp.float32)
        low = products[o] - high
        left_side[o] = jnp.concatenate([high, high, low], axis=0).T.astype(jnp.bfloat16)

    def counts(base, peer, entries):
        table = []
        for o in range(nb):
            row = []
            for r in range(nb):
                value = jnp.full((1, width), base, jnp.float32)
                if peer is not None:
                    mine = jnp.logical_and(send_ref[0, peer] == o, partner_ref[0, peer] == r)
                    got, for_mine = entries
                    theirs = jnp.logical_and(got == float(r), for_mine == float(o))
                    value = value + jnp.where(mine, 1.0, 0.0) + jnp.where(theirs, 1.0, 0.0)
                row.append(value)
            table.append(row)
        return table

    def fill_numer(slot, base, peer, source=None, place=None):
        entries = None
        if peer is not None:
            entries = [source[place, tail + used + e : tail + used + e + 1, :] for e in range(2)]
        table = counts(base, peer, entries)
        for o in range(nb):
            pieces = [held[slot, ROWS * r : ROWS * (r + 1), :] * table[o][r] for r in range(nb)]
            high, low = split(jnp.concatenate(pieces, axis=1))
            numer[slot, o] = jnp.dot(
                left_side[o],
                jnp.concatenate([high, low, high], axis=0),
                preferred_element_type=jnp.float32,
            )

    def spread_sources(slot, tile):
        for row in range(used):
            sources[slot, row] = jnp.broadcast_to(tile[row : row + 1], (8, width))

    def add_slots(members, first, unroll, step=None):
        def chunk(g, carry):
            part = pl.ds(pl.multiple_of(8 * g, 8), 8)
            mine = [at_i[row, part, :] for row in range(used)]
            if step is not None:
                mine = [mine[row] + step * vel_i[row, part, :] for row in range(used)]
            total = [None if first else acc[row, part, :] for row in range(used)]

            def add_one(slot, total):
                total = list(total)
                for r in range(nb):
                    theirs = [sources[slot, 3 * r + c] for c in range(3)]
                    for o in range(nb):
                        off = [mine[3 * o + c] - theirs[c] for c in range(3)]
                        square = CORE_SQUARE + off[0] * off[0] + off[1] * off[1] + off[2] * off[2]
                        inverse = lax.rsqrt(square)
                        weight = numer[slot, o, part, pl.ds(width * r, width)] * inverse * (inverse * inverse)
                        for c in range(3):
                            term = weight * off[c]
                            row = 3 * o + c
                            total[row] = term if total[row] is None else total[row] + term
                return total

            if members[1] - members[0] <= UNROLL_LIMIT:
                for slot in range(*members):
                    total = add_one(slot, total)
            else:
                if first:
                    total = [jnp.zeros((8, width), jnp.float32)] * used
                total = lax.fori_loop(members[0], members[1], add_one, total)
            for row in range(used):
                acc[row, part, :] = total[row]
            return carry

        lax.fori_loop(0, width // 8, chunk, 0, unroll=unroll)

    def velocity_of(position):
        sums = [jnp.sum(acc[row].T, axis=0, keepdims=True) for row in range(used)]
        pair = jnp.concatenate(sums + [jnp.zeros((8 - used, width), jnp.float32)], axis=0)
        before = jnp.where(lane == 0, position, pltpu.roll(position, 1, 1))
        after = jnp.where(lane == width - 1, position, pltpu.roll(position, width - 1, 1))
        chain = before + after - 2.0 * position
        force = COUPLE * pair + applied_ref[...] + TENSION * chain
        velocity = force / drag8_ref[...]
        square = velocity * velocity
        tops = []
        for o in range(nb):
            tops.append(square[3 * o : 3 * o + 1] + square[3 * o + 1 : 3 * o + 2] + square[3 * o + 2 : 3 * o + 3])
        return velocity, functools.reduce(jnp.maximum, tops)

    def step_length(row):
        top = jnp.max(row, axis=1, keepdims=True)
        return STEP_LENGTH / (jnp.sqrt(top) + EPSILON)

    fill_numer(0, 1.0, dom, stage, dom)
    spread_sources(0, position)
    add_slots((0, 1), True, 8)

    def from_sub(k, carry):
        sub_copy(k).wait_recv()
        fill_numer(k, 1.0, None)
        spread_sources(k, held[k, tail : tail + 8, :])
        return carry

    def from_dom(k, carry):
        slot = n_sub - 1 + k
        dom_copy(k).wait_recv()
        fill_numer(slot, 0.0, lax.rem(dom - k + n_dom, n_dom), held, slot)
        spread_sources(slot, held[slot, tail : tail + 8, :])
        return carry

    lax.fori_loop(1, n_sub, from_sub, 0)
    add_slots((1, n_sub), False, 4)
    lax.fori_loop(1, n_dom, from_dom, 0)
    add_slots((n_sub, slots), False, 4)
    velocity, top = velocity_of(position)
    vel_tx[...] = jnp.where(row_id == used, top, velocity)
    top1_tx[...] = top

    def vel_copy(slot, dom_to, sub_to):
        return pltpu.make_async_remote_copy(
            src_ref=vel_tx,
            dst_ref=vel_rx.at[slot],
            send_sem=vel_send,
            recv_sem=vel_recv,
            device_id=(dom_to, sub_to),
            device_id_type=MESH,
        )

    def top1_copy(index):
        kd, ks = index // (n_sub - 1) + 1, index % (n_sub - 1) + 1
        return pltpu.make_async_remote_copy(
            src_ref=top1_tx,
            dst_ref=top1_rx.at[index],
            send_sem=top1_send,
            recv_sem=top1_recv,
            device_id=(dom_id(kd), sub_id(ks)),
            device_id_type=MESH,
        )

    others = (n_sub - 1) * (n_dom - 1)
    repeat(1, n_dom, lambda k: vel_copy(n_sub - 1 + k, dom_id(k), sub).start())
    repeat(0, others, lambda k: top1_copy(k).start())
    repeat(1, n_sub, lambda k: vel_copy(k, dom, sub_id(k)).start())

    vel_rx[0] = vel_tx[...]
    spread(vel_i, velocity)

    arrived = vel_rx.at[pl.ds(1, slots - 1)]
    pltpu.make_async_copy(arrived, arrived, vel_recv).wait()
    pltpu.make_async_copy(top1_rx, top1_rx, top1_recv).wait()
    near = jnp.max(vel_rx[...], axis=0)[used : used + 1]
    far = jnp.max(top1_rx[...], axis=0)
    step = step_length(jnp.maximum(near, far))

    position = position + step * velocity

    def move(slot):
        spread_sources(slot, held[slot, tail : tail + 8, :] + step * vel_rx[slot])

    repeat(0, slots, move)
    add_slots((0, slots), True, 4, step)
    velocity, top = velocity_of(position)
    top2_tx[...] = top

    def top2_copy(index):
        kd, ks = (index + 1) // n_sub, (index + 1) % n_sub
        return pltpu.make_async_remote_copy(
            src_ref=top2_tx,
            dst_ref=top2_rx.at[index],
            send_sem=top2_send,
            recv_sem=top2_recv,
            device_id=(dom_id(kd), sub_id(ks)),
            device_id_type=MESH,
        )

    repeat(0, n_sub * n_dom - 1, lambda k: top2_copy(k).start())
    vel_ref[...] = velocity
    pos_ref[...] = position

    repeat(1, n_sub, lambda k: sub_copy(k).wait_send())
    repeat(1, n_dom, lambda k: dom_copy(k).wait_send())
    pltpu.make_async_copy(arrived, arrived, vel_send).wait()
    pltpu.make_async_copy(top1_rx, top1_rx, top1_send).wait()

    pltpu.make_async_copy(top2_rx, top2_rx, top2_recv).wait()
    top_ref[...] = jnp.maximum(jnp.max(top2_rx[...], axis=0), top)
    pltpu.make_async_copy(top2_rx, top2_rx, top2_send).wait()


def last_move(pos8_ref, vel8_ref, top_ref, pos_ref, vel_ref):
    _, nb, _ = pos_ref.shape
    step = STEP_LENGTH / (jnp.sqrt(jnp.max(top_ref[...], axis=1, keepdims=True)) + EPSILON)
    velocity = vel8_ref[...]
    position = pos8_ref[...] + step * velocity
    for o in range(nb):
        for c in range(3):
            vel_ref[c, o] = velocity[3 * o + c]
            pos_ref[c, o] = position[3 * o + c]


def solution(mesh):
    n_dom, n_sub = mesh.shape["dom"], mesh.shape["sub"]

    def local(segments, stress, drag_coef, send_ids, partner_ids):
        nb, _, width = segments.shape
        slots = n_sub + n_dom - 1
        rows = nb * ROWS + 8
        f32 = jnp.float32
        vmem = pl.BlockSpec(memory_space=pltpu.VMEM)
        out = jax.ShapeDtypeStruct((3, nb, width), f32)
        words = slots * nb * width * nb * width + (n_dom + slots) * rows * width + 10 * nb * width * width
        words += 64 * slots * width
        dma = pltpu.SemaphoreType.DMA
        tile = jax.ShapeDtypeStruct((8, width), f32)
        smem = pl.BlockSpec(memory_space=pltpu.SMEM)
        moved = pl.pallas_call(
            functools.partial(kernel, n_dom, n_sub),
            out_shape=(tile, tile, jax.ShapeDtypeStruct((1, width), f32)),
            in_specs=[vmem, vmem, smem, smem, smem],
            out_specs=(vmem, vmem, vmem),
            scratch_shapes=[
                pltpu.VMEM((n_dom, rows, width), f32),
                pltpu.VMEM((slots, rows, width), f32),
                pltpu.VMEM((slots, nb, width, nb * width), f32),
                pltpu.VMEM((nb, width, 3 * ROWS), jnp.bfloat16),
                pltpu.VMEM((3 * nb, width, width), f32),
                pltpu.VMEM((3 * nb, width, width), f32),
                pltpu.VMEM((3 * nb, width, width), f32),
                pltpu.VMEM((slots, 3 * nb, 8, width), f32),
                pltpu.VMEM((8, width), f32),
                pltpu.VMEM((8, width), f32),
                pltpu.VMEM((8, width), f32),
                pltpu.VMEM((slots, 8, width), f32),
                pltpu.VMEM((1, width), f32),
                pltpu.VMEM(((n_dom - 1) * (n_sub - 1), 1, width), f32),
                pltpu.VMEM((1, width), f32),
                pltpu.VMEM((n_dom * n_sub - 1, 1, width), f32),
                dma((slots,)),
                dma((slots,)),
                dma,
                dma,
                dma,
                dma,
                dma,
                dma,
            ],
            compiler_params=pltpu.CompilerParams(
                collective_id=0,
                has_side_effects=True,
                vmem_limit_bytes=4 * words + 8 * 1024 * 1024,
            ),
        )(
            segments,
            drag_coef,
            stress,
            send_ids.reshape(1, n_dom),
            partner_ids.reshape(1, n_dom),
        )
        position, velocity = pl.pallas_call(
            last_move,
            out_shape=(out, out),
            in_specs=[vmem, vmem, vmem],
            out_specs=(vmem, vmem),
        )(*moved)
        return position.transpose(1, 0, 2), velocity.transpose(1, 0, 2)

    in_specs = (
        P(("dom", "sub"), None, None),
        P(),
        P(("dom", "sub"), None),
        P(("dom", "sub"), None, None),
        P(("dom", "sub"), None, None),
    )
    out_specs = (P(("dom", "sub"), None, None), P(("dom", "sub"), None, None))
    return jax.shard_map(local, mesh=mesh, in_specs=in_specs, out_specs=out_specs, check_vma=False)
```

profile of v0, /device:TPU:0, one launch (start us, length us, event | category | flops | bytes accessed | tf_op | source)
XLA Modules:
  0.0 29.5 jit_solution(11302150676840888694)
XLA Ops:
  0.6 0.0 copy-start.2
  0.6 0.0 copy-start.3
  0.7 0.0 copy-start.4
  0.7 0.0 copy-start.5
  0.7 0.7 %copy.7.seg_ref = f32[2,9,128]{2,1,0:T(8,128)S(1)} copy(f32[2,9,128]{2,0,1:T(2,128)} %param.5) | data formatting | bytes 18432 | tf_op args[0]
  1.4 0.0 copy-done.2
  1.4 0.0 copy-done.3
  1.4 0.0 copy-done.4
  1.4 0.0 copy-done.5
  1.4 25.0 %shard_map.68 = (f32[8,128]{1,0:T(8,128)S(1)}, f32[8,128]{1,0:T(8,128)S(1)}, f32[1,128]{1,0:T(1,128)S(1)}) custom-call(f32[2,9,128]{2,1,0:T(8,128)S(1)} %copy.7.seg_ref, f32[2,128]{1,0:T(2,128)S(1)} %copy-done.3, f32[3,3]{1,0:T(4,128)S(1)} %copy-done.2, s32[1,8]{1,0:T(1,128)S(1)} %bitcast.4, s32[1,8]{1,0:T(1,128)S(1)} %bitcast.5), custom_call_target="tpu_custom_call" | custom-call | tf_op jit(solution)/shard_map/pallas_call | solution.py:380
  26.4 0.0 copy-start
  26.4 0.6 %copy-done = f32[8,128]{1,0:T(8,128)} copy-done((f32[8,128]{1,0:T(8,128)}, f32[8,128]{1,0:T(8,128)S(1)}, u32[]{:S(2)}) %copy-start) | copy-done | bytes 4120
  27.0 0.0 copy-start.1
  27.0 0.6 %copy-done.1 = f32[8,128]{1,0:T(8,128)} copy-done((f32[8,128]{1,0:T(8,128)}, f32[8,128]{1,0:T(8,128)S(1)}, u32[]{:S(2)}) %copy-start.1) | copy-done | bytes 4120
  27.6 0.0 copy-start.6
  27.6 0.5 %copy-done.6 = f32[1,128]{1,0:T(1,128)} copy-done((f32[1,128]{1,0:T(1,128)}, f32[1,128]{1,0:T(1,128)S(1)}, u32[]{:S(2)}) %copy-start.6) | copy-done | bytes 536
  28.1 1.4 %shard_map.69 = (f32[3,2,128]{2,1,0:T(2,128)}, f32[3,2,128]{2,1,0:T(2,128)}) custom-call(f32[8,128]{1,0:T(8,128)} %copy-done, f32[8,128]{1,0:T(8,128)} %copy-done.1, f32[1,128]{1,0:T(1,128)} %copy-done.6), custom_call_target="tpu_custom_call" | custom-call | tf_op jit(solution)/shard_map/pallas_call | solution.py:423
Async XLA Ops:
  0.6 0.8 %copy-start.2 = (f32[3,3]{1,0:T(4,128)S(1)}, f32[3,3]{1,0:T(4,128)}, u32[]{:S(2)}) copy-start(f32[3,3]{1,0:T(4,128)} %stress_ref.1) | copy-start | bytes 112
  0.6 0.8 %copy-start.3 = (f32[2,128]{1,0:T(2,128)S(1)}, f32[2,128]{1,0:T(2,128)}, u32[]{:S(2)}) copy-start(f32[2,128]{1,0:T(2,128)} %drag_ref.1) | copy-start | bytes 3076
  0.7 0.8 %copy-start.4 = (s32[1,8,1]{1,2,0:T(1,128)S(1)}, s32[1,8,1]{1,2,0:T(1,128)}, u32[]{:S(2)}) copy-start(s32[1,8,1]{1,2,0:T(1,128)} %param.8) | copy-start | bytes 100
  0.7 0.7 %copy-start.5 = (s32[1,8,1]{1,2,0:T(1,128)S(1)}, s32[1,8,1]{1,2,0:T(1,128)}, u32[]{:S(2)}) copy-start(s32[1,8,1]{1,2,0:T(1,128)} %param.9) | copy-start | bytes 100
  26.4 0.6 %copy-start = (f32[8,128]{1,0:T(8,128)}, f32[8,128]{1,0:T(8,128)S(1)}, u32[]{:S(2)}) copy-start(f32[8,128]{1,0:T(8,128)S(1)} %get-tuple-element.7.pos8_ref) | copy-start | bytes 12292
  27.0 0.6 %copy-start.1 = (f32[8,128]{1,0:T(8,128)}, f32[8,128]{1,0:T(8,128)S(1)}, u32[]{:S(2)}) copy-start(f32[8,128]{1,0:T(8,128)S(1)} %get-tuple-element.8.vel8_ref) | copy-start | bytes 12292
  27.6 0.5 %copy-start.6 = (f32[1,128]{1,0:T(1,128)}, f32[1,128]{1,0:T(1,128)S(1)}, u32[]{:S(2)}) copy-start(f32[1,128]{1,0:T(1,128)S(1)} %get-tuple-element.9.top_ref) | copy-start | bytes 1540
where the time goes:
time: 29.7 us; the launch traced here: 29.5 us
  Pallas kernels  26.3 us (89%)
  local copies, waits for them, and re-layouts  2.45 us (8%)
  between operations  0.69 us (2%)
    pallas_call x1, Pallas kernels, local(): pl.pallas_call(functools.partial(kernel, n_dom, n_sub), out_shape=(tile,...  25 us
    unnamed x15, local copies, waits for them, and re-layouts  2.45 us
    pallas_call x1, Pallas kernels, local(): pl.pallas_call(last_move, out_shape=(out, out), in_specs=[vmem, vmem, vme...  1.36 us

commit v1 on v0

--- a/solution.py
+++ b/solution.py
@@ -16,7 +16,7 @@
 
 MESH = pl.DeviceIdType.MESH
 ROWS = 16
-UNROLL_LIMIT = 64
+UNROLL_LIMIT = 16
 
 
 def repeat(first, last, body):
@@ -42,7 +42,6 @@
     partner_ref,
     pos_ref,
     vel_ref,
-    top_ref,
     stage,
     held,
     numer,
@@ -257,7 +256,7 @@
 
     fill_numer(0, 1.0, dom, stage, dom)
     spread_sources(0, position)
-    add_slots((0, 1), True, 8)
+    add_slots((0, 1), True, 2)
 
     def from_sub(k, carry):
         sub_copy(k).wait_recv()
@@ -273,9 +272,9 @@
         return carry
 
     lax.fori_loop(1, n_sub, from_sub, 0)
-    add_slots((1, n_sub), False, 4)
+    add_slots((1, n_sub), False, 1)
     lax.fori_loop(1, n_dom, from_dom, 0)
-    add_slots((n_sub, slots), False, 4)
+    add_slots((n_sub, slots), False, 1)
     velocity, top = velocity_of(position)
     vel_tx[...] = jnp.where(row_id == used, top, velocity)
     top1_tx[...] = top
@@ -291,7 +290,7 @@
         )
 
     def top1_copy(index):
-        kd, ks = index // (n_sub - 1) + 1, index % (n_sub - 1) + 1
+        kd, ks = lax.div(index, n_sub - 1) + 1, lax.rem(index, n_sub - 1) + 1
         return pltpu.make_async_remote_copy(
             src_ref=top1_tx,
             dst_ref=top1_rx.at[index],
@@ -322,12 +321,12 @@
         spread_sources(slot, held[slot, tail : tail + 8, :] + step * vel_rx[slot])
 
     repeat(0, slots, move)
-    add_slots((0, slots), True, 4, step)
+    add_slots((0, slots), True, 1, step)
     velocity, top = velocity_of(position)
     top2_tx[...] = top
 
     def top2_copy(index):
-        kd, ks = (index + 1) // n_sub, (index + 1) % n_sub
+        kd, ks = lax.div(index + 1, n_sub), lax.rem(index + 1, n_sub)
         return pltpu.make_async_remote_copy(
             src_ref=top2_tx,
             dst_ref=top2_rx.at[index],
@@ -338,8 +337,8 @@
         )
 
     repeat(0, n_sub * n_dom - 1, lambda k: top2_copy(k).start())
-    vel_ref[...] = velocity
-    pos_ref[...] = position
+    for o in range(nb):
+        vel_ref[o] = velocity[3 * o : 3 * o + 3]
 
     repeat(1, n_sub, lambda k: sub_copy(k).wait_send())
     repeat(1, n_dom, lambda k: dom_copy(k).wait_send())
@@ -347,19 +346,11 @@
     pltpu.make_async_copy(top1_rx, top1_rx, top1_send).wait()
 
     pltpu.make_async_copy(top2_rx, top2_rx, top2_recv).wait()
-    top_ref[...] = jnp.maximum(jnp.max(top2_rx[...], axis=0), top)
+    step = step_length(jnp.maximum(jnp.max(top2_rx[...], axis=0), top))
+    position = position + step * velocity
+    for o in range(nb):
+        pos_ref[o] = position[3 * o : 3 * o + 3]
     pltpu.make_async_copy(top2_rx, top2_rx, top2_send).wait()
-
-
-def last_move(pos8_ref, vel8_ref, top_ref, pos_ref, vel_ref):
-    _, nb, _ = pos_ref.shape
-    step = STEP_LENGTH / (jnp.sqrt(jnp.max(top_ref[...], axis=1, keepdims=True)) + EPSILON)
-    velocity = vel8_ref[...]
-    position = pos8_ref[...] + step * velocity
-    for o in range(nb):
-        for c in range(3):
-            vel_ref[c, o] = velocity[3 * o + c]
-            pos_ref[c, o] = position[3 * o + c]
 
 
 def solution(mesh):
@@ -371,17 +362,16 @@
         rows = nb * ROWS + 8
         f32 = jnp.float32
         vmem = pl.BlockSpec(memory_space=pltpu.VMEM)
-        out = jax.ShapeDtypeStruct((3, nb, width), f32)
+        out = jax.ShapeDtypeStruct((nb, 3, width), f32)
         words = slots * nb * width * nb * width + (n_dom + slots) * rows * width + 10 * nb * width * width
         words += 64 * slots * width
         dma = pltpu.SemaphoreType.DMA
-        tile = jax.ShapeDtypeStruct((8, width), f32)
         smem = pl.BlockSpec(memory_space=pltpu.SMEM)
-        moved = pl.pallas_call(
+        return pl.pallas_call(
             functools.partial(kernel, n_dom, n_sub),
-            out_shape=(tile, tile, jax.ShapeDtypeStruct((1, width), f32)),
+            out_shape=(out, out),
             in_specs=[vmem, vmem, smem, smem, smem],
-            out_specs=(vmem, vmem, vmem),
+            out_specs=(vmem, vmem),
             scratch_shapes=[
                 pltpu.VMEM((n_dom, rows, width), f32),
                 pltpu.VMEM((slots, rows, width), f32),
@@ -420,13 +410,6 @@
             send_ids.reshape(1, n_dom),
             partner_ids.reshape(1, n_dom),
         )
-        position, velocity = pl.pallas_call(
-            last_move,
-            out_shape=(out, out),
-            in_specs=[vmem, vmem, vmem],
-            out_specs=(vmem, vmem),
-        )(*moved)
-        return position.transpose(1, 0, 2), velocity.transpose(1, 0, 2)
 
     in_specs = (
         P(("dom", "sub"), None, None),

time: 29.7 us -> 28.4 us (0.956)
  Pallas kernels: 26.3 us -> 25.6 us
  local copies, waits for them, and re-layouts: 2.45 us -> 1.9 us
    unnamed x15 -> x9, local copies, waits for them, and re-layouts: 2.45 us -> 0.74 us
    pallas_call x0 -> x2, local copies, waits for them, and re-layouts: none -> 1.16 us  [local(): pl.pallas_call(functools.partial(kernel, n_dom, n_sub), out_shape=(out, o...]
    pallas_call x2 -> x1, Pallas kernels: 26.3 us -> 25.6 us  [local(): pl.pallas_call(functools.partial(kernel, n_dom, n_sub), out_shape=(out, o...]
where the time goes in v1:
time: 28.4 us; the launch traced here: 28.2 us
  Pallas kernels  25.6 us (90%)
  local copies, waits for them, and re-layouts  1.9 us (7%)
  between operations  0.68 us (2%)
    pallas_call x1, Pallas kernels, local(): pl.pallas_call(functools.partial(kernel, n_dom, n_sub), out_shape=(out, o...  25.6 us
    pallas_call x2, local copies, waits for them, and re-layouts, local(): pl.pallas_call(functools.partial(kernel, n_dom, n_sub), out_shape=(out, o...  1.16 us
    unnamed x9, local copies, waits for them, and re-layouts  0.74 us

profile of v1, /device:TPU:0, one launch (start us, length us, event | category | flops | bytes accessed | tf_op | source)
XLA Modules:
  0.0 28.2 jit_solution(2652306102805587277)
XLA Ops:
  0.6 0.0 copy-start
  0.6 0.0 copy-start.1
  0.7 0.0 copy-start.2
  0.7 0.0 copy-start.3
  0.7 0.7 %copy.7.seg_ref = f32[2,9,128]{2,1,0:T(8,128)S(1)} copy(f32[2,9,128]{2,0,1:T(2,128)} %param.5) | data formatting | bytes 18432 | tf_op args[0]
  1.4 0.0 copy-done
  1.4 0.0 copy-done.1
  1.4 0.0 copy-done.2
  1.4 0.0 copy-done.3
  1.4 25.6 %shard_map.68 = (f32[2,3,128]{2,1,0:T(4,128)S(1)}, f32[2,3,128]{2,1,0:T(4,128)S(1)}) custom-call(f32[2,9,128]{2,1,0:T(8,128)S(1)} %copy.7.seg_ref, f32[2,128]{1,0:T(2,128)S(1)} %copy-done.1, f32[3,3]{1,0:T(4,128)S(1)} %copy-done, s32[1,8]{1,0:T(1,128)S(1)} %bitcast.2, s32[1,8]{1,0:T(1,128)S(1)} %bitcast.3), custom_call_target="tpu_custom_call" | custom-call | tf_op jit(solution)/shard_map/pallas_call | solution.py:370
  27.0 0.6 %copy.8 = f32[2,3,128]{2,0,1:T(2,128)} copy(f32[2,3,128]{2,1,0:T(4,128)S(1)} %get-tuple-element.2) | data formatting | bytes 6144 | tf_op jit(solution)/shard_map/pallas_call | solution.py:370
  27.6 0.6 %copy.9 = f32[2,3,128]{2,0,1:T(2,128)} copy(f32[2,3,128]{2,1,0:T(4,128)S(1)} %get-tuple-element.3) | data formatting | bytes 6144 | tf_op jit(solution)/shard_map/pallas_call | solution.py:370
Async XLA Ops:
  0.6 0.8 %copy-start = (f32[3,3]{1,0:T(4,128)S(1)}, f32[3,3]{1,0:T(4,128)}, u32[]{:S(2)}) copy-start(f32[3,3]{1,0:T(4,128)} %stress_ref.1) | copy-start | bytes 112
  0.6 0.8 %copy-start.1 = (f32[2,128]{1,0:T(2,128)S(1)}, f32[2,128]{1,0:T(2,128)}, u32[]{:S(2)}) copy-start(f32[2,128]{1,0:T(2,128)} %drag_ref.1) | copy-start | bytes 3076
  0.7 0.8 %copy-start.2 = (s32[1,8,1]{1,2,0:T(1,128)S(1)}, s32[1,8,1]{1,2,0:T(1,128)}, u32[]{:S(2)}) copy-start(s32[1,8,1]{1,2,0:T(1,128)} %param.8) | copy-start | bytes 100
  0.7 0.7 %copy-start.3 = (s32[1,8,1]{1,2,0:T(1,128)S(1)}, s32[1,8,1]{1,2,0:T(1,128)}, u32[]{:S(2)}) copy-start(s32[1,8,1]{1,2,0:T(1,128)} %param.9) | copy-start | bytes 100
